TPU v7x, 32 devices: a whole 2x2x4 slice. The times are simulated.
32 devices in a mesh: row: 4 (over y, x), col: 8 (over z, core).
Axes of the slice: x: 2, y: 2, z: 4, core: 2. Of those that a mesh axis runs over, the one named last changes fastest.
Arguments:
- latent: bfloat16 [64, 64, 256], P('row', 'col'), may hold values from -6 to 6
- well_logs: bfloat16 [32, 256], P(('row', 'col')), may hold values from -6 to 6
- cond_weight: bfloat16 [256, 256], replicated, may hold values from -0.375 to 0.375
- trace_rows: int32 [64], P('col'), may hold values from 0 to 31, as said below
- norm_gain: float32 [256], replicated, may hold values from 0.5 to 1.5
- in_weight: bfloat16 [256, 512], replicated, may hold values from -0.375 to 0.375
- conv_weight: float32 [9, 256], replicated, may hold values from -2 to 2
- bc_weight: bfloat16 [256, 1024], replicated, may hold values from -0.375 to 0.375
- dt_weight: bfloat16 [256, 64], replicated, may hold values from -0.375 to 0.375
- dt_bias: float32 [4, 16], replicated, may hold values from -0.5 to 0.5
- row_rate: float32 [2, 16], replicated, may hold values from 1 to 512
- col_rate: float32 [2, 16], replicated, may hold values from 1 to 512
- horizon: float32 [64, 64], P('row', 'col'), may hold values from 0 to 1
- out_gain: float32 [256], replicated, may hold values from 0.5 to 1.5
- out_weight: bfloat16 [256, 256], replicated, may hold values from -0.375 to 0.375
Outputs:
- block_out: bfloat16 [64, 64, 256], P('row', 'col')
Inputs may be any that keep to these rules, and one draw needn't show every extreme that they name: `trace_rows`: every conditioning token row is named by some plane column.
All inputs are finite; a program needn't handle non-finite values.
Results may differ from a plain program's by a relative error of at most 0.009.
Values may be sent and summed in bfloat16 or wider, within the bound.
A program may use at most 192 MiB of HBM per device.

v0:
```python
import jax
import jax.numpy as jnp
from jax import lax
from jax.sharding import PartitionSpec as P

precise = lax.Precision.HIGHEST


def padded_2(cells, sides, width):
    for axis, dim in sides:
        count = lax.axis_size(axis)
        ends = count - 1
        head = lax.slice_in_dim(cells, 0, width, axis=dim)
        tail = lax.slice_in_dim(cells, cells.shape[dim] - width, cells.shape[dim], axis=dim)
        cells = jnp.concatenate(
            [
                lax.ppermute(tail, axis, [(i, (i + 1) % count) for i in range(ends)]),
                cells,
                lax.ppermute(head, axis, [((i + 1) % count, i) for i in range(ends)]),
            ],
            axis=dim,
        )
    return cells


def entering(array, axis, join, neutral, backward):
    count = lax.axis_size(axis)
    place = lax.axis_index(axis)
    ahead = count - 1 - place if backward else place
    gathered = jax.tree.map(
        lambda a, kind: lax.all_gather(a.astype(kind), axis), array, (jnp.bfloat16, jnp.bfloat16)
    )
    state = jax.tree.map(lambda a, e: jnp.zeros_like(a) + jnp.asarray(e, a.dtype), array, neutral)

    def one(turn, state):
        source = count - 1 - turn if backward else turn
        return join(
            state,
            jax.tree.map(
                lambda a, own: lax.dynamic_index_in_dim(a, source, 0, False).astype(own.dtype),
                gathered,
                array,
            ),
        )

    return lax.fori_loop(0, ahead, one, state)


def segment_recurrence(states, pieces):
    signal, in_coef, out_coef, step_size, log_decay = pieces
    block_len = signal.shape[1]
    cumulative = jnp.cumsum(log_decay, axis=1)
    scores = jnp.einsum("lks,ljs->lkj", out_coef, in_coef, preferred_element_type=jnp.float32)
    driven = signal.astype(jnp.float32) * step_size[..., None]
    causal = jnp.arange(block_len)[:, None] >= jnp.arange(block_len)[None, :]

    def head_term(head_args):
        head_cum, head_drive = head_args
        spread = jnp.where(causal, head_cum[:, :, None] - head_cum[:, None, :], -jnp.inf)
        return jnp.einsum("lkj,ljp->lkp", scores * jnp.exp(spread), head_drive, precision=precise)

    inner = lax.map(head_term, (jnp.moveaxis(cumulative, 2, 0), jnp.moveaxis(driven, 2, 0)))
    inner = jnp.moveaxis(inner, 0, 2)
    carried_in = jnp.exp(cumulative)[..., None] * jnp.einsum(
        "lks,lhps->lkhp", out_coef.astype(jnp.float32), states, precision=precise
    )
    tail_decay = jnp.exp(cumulative[:, -1:, :] - cumulative)
    states = jnp.exp(cumulative[:, -1, :])[:, :, None, None] * states + jnp.einsum(
        "lkhp,lks->lhps",
        driven * tail_decay[..., None],
        in_coef.astype(jnp.float32),
        precision=precise,
    )
    output = inner + carried_in
    return (states, output.reshape(output.shape[0], block_len, -1))


def line_scan(signal, in_coef, out_coef, step_size, log_decay, states):
    line_count = signal.shape[0]
    length = signal.shape[1]
    block_len = min(64, length)
    blocks = length // block_len

    def split_blocks(array):
        shaped = array.reshape((line_count, blocks, block_len) + array.shape[2:])
        return jnp.moveaxis(shaped, 1, 0)

    pieces = (
        split_blocks(signal),
        split_blocks(in_coef),
        split_blocks(out_coef),
        split_blocks(step_size),
        split_blocks(log_decay),
    )
    states, outputs = lax.scan(segment_recurrence, states, pieces)
    outputs = jnp.moveaxis(outputs, 0, 1).reshape(line_count, length, -1)
    return (outputs, states)


def orient(array, along_columns, backward):
    if along_columns:
        array = jnp.swapaxes(array, 0, 1)
    if backward:
        array = jnp.flip(array, 1)
    return array


def restore(array, along_columns, backward):
    if backward:
        array = jnp.flip(array, 1)
    if along_columns:
        array = jnp.swapaxes(array, 0, 1)
    return array


def direction_inputs(mixed, marks, bc_weight, dt_weight, dt_bias, rate_row, line_length, direction):
    tile_shape = mixed.shape[:2]
    inner_width = mixed.shape[2]
    head_count = dt_bias.shape[1]
    state_dim = bc_weight.shape[1] // 8
    flat_x = mixed.reshape(-1, inner_width)
    coef_pair = (
        jnp.dot(
            flat_x,
            bc_weight[:, direction * 2 * state_dim : (direction + 1) * 2 * state_dim],
            preferred_element_type=jnp.float32,
        )
        .astype(jnp.bfloat16)
        .reshape(tile_shape + (2 * state_dim,))
    )
    step_size = jax.nn.softplus(
        jnp.dot(
            flat_x,
            dt_weight[:, direction * head_count : (direction + 1) * head_count],
            preferred_element_type=jnp.float32,
        ).reshape(tile_shape + (head_count,))
        + dt_bias[direction]
    )
    log_decay = -step_size * (rate_row / (16.0 * line_length)) - marks[:, :, None]
    signal = mixed.reshape(tile_shape + (head_count, inner_width // head_count))
    return (signal, coef_pair[..., :state_dim], coef_pair[..., state_dim:], step_size, log_decay)


def oriented_scan(inputs, along_columns, backward):
    signal_l = orient(inputs[0], along_columns, backward)
    in_l = orient(inputs[1], along_columns, backward)
    out_l = orient(inputs[2], along_columns, backward)
    step_l = orient(inputs[3], along_columns, backward)
    decay_l = orient(inputs[4], along_columns, backward)
    zero_states = jnp.zeros(
        (signal_l.shape[0], signal_l.shape[2], signal_l.shape[3], in_l.shape[2]), jnp.float32
    )
    outputs, states = line_scan(signal_l, in_l, out_l, step_l, decay_l, zero_states)
    cumulative = jnp.cumsum(decay_l, axis=1)
    return (outputs, states, jnp.exp(cumulative[:, -1, :]), cumulative, out_l)


def finish(outputs, cumulative, out_l, inflow, along_columns, backward):
    extra = jnp.exp(cumulative)[..., None] * jnp.einsum(
        "lks,lhps->lkhp", out_l.astype(jnp.float32), inflow, precision=precise
    )
    return restore(outputs + extra.reshape(outputs.shape), along_columns, backward)


def combine_states(earlier, later):
    return (earlier[0] * later[0], later[0][:, :, None, None] * earlier[1] + later[1])


def per_device(
    latent,
    well_logs,
    cond_weight,
    trace_rows,
    norm_gain,
    in_weight,
    conv_weight,
    bc_weight,
    dt_weight,
    dt_bias,
    row_rate,
    col_rate,
    horizon,
    out_gain,
    out_weight,
):
    tile_rows, tile_cols, width = latent.shape
    inner_width = in_weight.shape[1] // 2
    row_length = tile_cols * lax.axis_size("col")
    col_length = tile_rows * lax.axis_size("row")
    local_tokens = jax.nn.silu(
        jnp.dot(well_logs, cond_weight, preferred_element_type=jnp.float32)
    ).astype(jnp.bfloat16)
    shard_rows = lax.all_gather(local_tokens, ("row", "col"), axis=0, tiled=True)
    positions = jnp.arange(shard_rows.shape[0])[None, :]
    select = (trace_rows[:, None] == positions).astype(jnp.bfloat16)
    column_tokens = jnp.dot(select, shard_rows, preferred_element_type=jnp.float32)
    hidden = latent.astype(jnp.float32) + column_tokens[None, :, :]
    normed = (
        hidden * lax.rsqrt(jnp.mean(hidden * hidden, axis=-1, keepdims=True) + 1e-06) * norm_gain
    ).astype(jnp.bfloat16)
    projected = (
        jnp.dot(normed.reshape(-1, width), in_weight, preferred_element_type=jnp.float32)
        .astype(jnp.bfloat16)
        .reshape(tile_rows, tile_cols, 2 * inner_width)
    )
    pre_conv = projected[..., :inner_width]
    gating_share = projected[..., inner_width:]
    padded = padded_2(pre_conv, (("row", 0), ("col", 1)), 1)
    conv_sum = jnp.zeros((tile_rows, tile_cols, inner_width), jnp.float32)
    for offset_row in range(3):
        for offset_col in range(3):
            conv_sum = (
                conv_sum
                + padded[
                    offset_row : offset_row + tile_rows, offset_col : offset_col + tile_cols
                ].astype(jnp.float32)
                * conv_weight[3 * offset_row + offset_col]
            )
    mixed_x = jax.nn.silu(conv_sum).astype(jnp.bfloat16)
    ahead = oriented_scan(
        direction_inputs(
            mixed_x, horizon, bc_weight, dt_weight, dt_bias, row_rate[0], row_length, 0
        ),
        False,
        False,
    )
    inflow_ahead = entering(
        (ahead[2], ahead[1]),
        "col",
        combine_states,
        (jnp.ones_like(ahead[2]), jnp.zeros_like(ahead[1])),
        False,
    )[1]
    behind = oriented_scan(
        direction_inputs(
            mixed_x, horizon, bc_weight, dt_weight, dt_bias, row_rate[1], row_length, 1
        ),
        False,
        True,
    )
    inflow_behind = entering(
        (behind[2], behind[1]),
        "col",
        combine_states,
        (jnp.ones_like(behind[2]), jnp.zeros_like(behind[1])),
        True,
    )[1]
    row_total = finish(ahead[0], ahead[3], ahead[4], inflow_ahead, False, False) + finish(
        behind[0], behind[3], behind[4], inflow_behind, False, True
    )
    ahead = oriented_scan(
        direction_inputs(
            mixed_x, horizon, bc_weight, dt_weight, dt_bias, col_rate[0], col_length, 2
        ),
        True,
        False,
    )
    inflow_ahead = entering(
        (ahead[2], ahead[1]),
        "row",
        combine_states,
        (jnp.ones_like(ahead[2]), jnp.zeros_like(ahead[1])),
        False,
    )[1]
    behind = oriented_scan(
        direction_inputs(
            mixed_x, horizon, bc_weight, dt_weight, dt_bias, col_rate[1], col_length, 3
        ),
        True,
        True,
    )
    inflow_behind = entering(
        (behind[2], behind[1]),
        "row",
        combine_states,
        (jnp.ones_like(behind[2]), jnp.zeros_like(behind[1])),
        True,
    )[1]
    col_total = finish(ahead[0], ahead[3], ahead[4], inflow_ahead, True, False) + finish(
        behind[0], behind[3], behind[4], inflow_behind, True, True
    )
    total = row_total + col_total
    gated = (
        total
        * lax.rsqrt(jnp.mean(total * total, axis=-1, keepdims=True) + 1e-05)
        * out_gain
        * jax.nn.silu(gating_share.astype(jnp.float32))
    ).astype(jnp.bfloat16)
    branch = jnp.dot(
        gated.reshape(-1, inner_width), out_weight, preferred_element_type=jnp.float32
    ).reshape(tile_rows, tile_cols, width)
    return (hidden + branch).astype(jnp.bfloat16)


def solution(mesh):
    placed = (
        P("row", "col", None),
        P(("row", "col"), None),
        P(),
        P("col"),
        P(),
        P(),
        P(),
        P(),
        P(),
        P(),
        P(),
        P(),
        P("row", "col"),
        P(),
        P(),
    )
    return jax.shard_map(
        per_device, mesh=mesh, in_specs=placed, out_specs=P("row", "col", None), check_vma=False
    )
```

profile of v0, /device:TPU:0, one launch (start us, length us, event | category | flops | bytes accessed | tf_op | source)
XLA Modules:
  0.0 356.0 jit_solution(13191213852494320829)
XLA Ops:
  7.7 43.3 %all-gather.9 = bf16[32,1,256]{2,1,0:T(2,128)(2,1)S(1)} all-gather(bf16[1,1,256]{2,1,0:T(2,128)(2,1)S(1)} %reshape.389), channel_id=2, replica_groups=mesh['row'=4,'col'=8] {'row','col'}, dimensions={0}, use_global_device_ids=true | all-gather | bytes 16896 | tf_op jit(solution)/shard_map/all_gather | solution.py:193
  53.9 1.3 collective-permute-start.1
  55.2 4.5 %collective-permute-start = (bf16[1,8,256]{2,1,0:T(8,128)(2,1)S(1)}, bf16[1,8,256]{2,1,0:T(8,128)(2,1)S(1)}, u32[]{:S(2)}, u32[]{:S(2)}) collective-permute-start(bf16[1,8,256]{2,1,0:T(8,128)(2,1)S(1)} %get-tuple-element.726), channel_id=1, source_target_pairs={{0,8},{8,16},{16,24},{1,9},{9,17},{17,25},{2,10},{10,18},{18,26},{... | collective-permute-start | bytes 12296 | tf_op jit(solution)/shard_map/ppermute | solution.py:17
  60.7 1.4 multiply_bitcast_fusion.2
  62.2 1.7 collective-permute-start.2
  63.9 1.3 collective-permute-start.3
  71.3 6.2 %while.134 = (s32[]{:T(128)}, f32[16,8,16,16]{3,2,0,1:T(8,128)S(1)}, f32[16,8,16]{2,1,0:T(8,128)S(1)}, f32[8,16,16]{2,1,0:T(8,128)S(1)}, f32[16,8,16,16]{3,0,1,2:T(8,128)S(1)}, /*index=5*/s32[]{:T(128)}) while((s32[]{:T(128)}, f32[16,8,16,16]{3,2,0,1:T(8,128)S(1)}, f32[16,8,16]{2,1,0:T(8,128)S(1)}, f32[8,16,16]{2,1,0:T(8,128)S(1)}, ...), condition=%wide.region_13.14_spmd.clone, body=%wide.region_12.13_spmd.clone.sunk | while | flops 399618 | bytes 224601 | solution.py:62
  78.3 2.2 fusion.56
  86.3 1.5 fusion.72
  87.9 2.2 fusion.57
  94.9 7.9 %all-gather.5 = bf16[32,1,16]{2,0,1:T(8,128)(2,1)} all-gather(bf16[8,1,16]{2,0,1:T(8,128)(2,1)S(1)} %get-tuple-element.753), channel_id=7, replica_groups=mesh['row'=4,'col'=8] {'row'}, dimensions={0}, use_global_device_ids=true | all-gather | bytes 1280 | tf_op jit(solution)/shard_map/all_gather | solution.py:31
  102.8 8.4 %all-gather.7 = bf16[32,1,16]{2,0,1:T(8,128)(2,1)} all-gather(bf16[8,1,16]{2,0,1:T(8,128)(2,1)S(1)} %get-tuple-element.745), channel_id=9, replica_groups=mesh['row'=4,'col'=8] {'row'}, dimensions={0}, use_global_device_ids=true | all-gather | bytes 1280 | tf_op jit(solution)/shard_map/all_gather | solution.py:31
  111.2 14.9 %all-gather.1 = bf16[128,1,16]{2,0,1:T(8,128)(2,1)} all-gather(bf16[16,1,16]{2,0,1:T(8,128)(2,1)S(1)} %get-tuple-element.741), channel_id=3, replica_groups=mesh['row'=4,'col'=8] {'col'}, dimensions={0}, use_global_device_ids=true | all-gather | bytes 4608 | tf_op jit(solution)/shard_map/all_gather | solution.py:31
  126.1 15.0 %all-gather.3 = bf16[128,1,16]{2,0,1:T(8,128)(2,1)} all-gather(bf16[16,1,16]{2,0,1:T(8,128)(2,1)S(1)} %get-tuple-element.735), channel_id=5, replica_groups=mesh['row'=4,'col'=8] {'col'}, dimensions={0}, use_global_device_ids=true | all-gather | bytes 4608 | tf_op jit(solution)/shard_map/all_gather | solution.py:31
  143.2 2.2 fusion.74
  145.3 3.0 add_convert_fusion.1
  148.3 1.2 fusion.51
  150.5 3.8 %add_convert_fusion = bf16[16,16,16,128]{3,2,1,0:T(8,128)(2,1)} fusion(f32[16,8,16,16]{3,2,1,0:T(8,128)S(1)} %get-tuple-element.718, f32[16,16]{1,0:T(8,128)S(1)} %exponential_multiply_fusion, bf16[16,8,128]{2,1,0:T(8,128)(2,1)} %rev.46), kind=kOutput, calls=%fused_computation.70 | convolution fusion | flops 51380224 | bytes 1213440 | tf_op jit(solution)/shard_map/while/body/eval_jaxpr/lkhp,lks->lhps/dot_general | solution.py:68
  154.4 33.5 %while.135 = (s32[]{:T(128)}, f32[16,8,16,16]{3,2,0,1:T(8,128)S(1)}, f32[16,8,16]{2,1,0:T(8,128)}, f32[8,16,16]{2,1,0:T(8,128)S(1)}, f32[16,8,16,16]{3,0,1,2:T(8,128)}, /*index=5*/s32[]{:T(128)}) while((s32[]{:T(128)}, f32[16,8,16,16]{3,2,0,1:T(8,128)S(1)}, f32[16,8,16]{2,1,0:T(8,128)}, f32[8,16,16]{2,1,0:T(8,128)S(1)}, ...), condition=%wide.region_18.19_spmd.clone, body=%wide.region_17.18_spmd.clone.sunk | while | flops 399618 | bytes 224601 | solution.py:62
  160.6 1.2 constant_dynamic-slice_fusion.11
  162.8 1.1 constant_dynamic-slice_fusion.11
  179.5 1.1 constant_dynamic-slice_fusion.11
  187.9 1.3 fusion.49
  189.2 48.9 %while.132 = (s32[]{:T(128)}, f32[16,16,8,16]{3,2,0,1:T(8,128)S(1)}, f32[16,16,8]{1,2,0:T(8,128)}, f32[16,8,8]{2,1,0:T(8,128)}, f32[16,16,8,16]{3,0,2,1:T(8,128)}, /*index=5*/s32[]{:T(128)}) while((s32[]{:T(128)}, f32[16,16,8,16]{3,2,0,1:T(8,128)S(1)}, f32[16,16,8]{1,2,0:T(8,128)}, f32[16,8,8]{2,1,0:T(8,128)}, ...), condition=%wide.region_3.4_spmd.clone, body=%wide.region_2.3_spmd.clone.sunk | while | flops 199746 | bytes 171161 | solution.py:62
  189.2 1.1 constant_dynamic-slice_fusion.8
  191.2 1.2 fusion.206
  194.2 1.2 fusion.206
  197.3 1.2 fusion.206
  200.3 1.2 fusion.206
  203.4 1.2 fusion.206
  206.4 1.2 fusion.206
  209.5 1.2 fusion.206
  212.5 1.2 fusion.206
  215.6 1.2 fusion.206
  218.6 1.2 fusion.206
  221.7 1.2 fusion.206
  224.7 1.2 fusion.206
  227.8 1.2 fusion.206
  230.8 1.2 fusion.206
  233.9 1.2 fusion.206
  236.9 1.2 fusion.206
  238.1 2.6 fusion.55
  240.8 35.5 %while.133 = (s32[]{:T(128)}, f32[16,16,8,16]{3,2,0,1:T(8,128)S(1)}, f32[16,16,8]{1,2,0:T(8,128)}, f32[16,8,8]{2,1,0:T(8,128)S(1)}, f32[16,16,8,16]{3,0,2,1:T(8,128)}, /*index=5*/s32[]{:T(128)}) while((s32[]{:T(128)}, f32[16,16,8,16]{3,2,0,1:T(8,128)S(1)}, f32[16,16,8]{1,2,0:T(8,128)}, f32[16,8,8]{2,1,0:T(8,128)S(1)}, ...), condition=%wide.region_8.9_spmd.clone, body=%wide.region_7.8_spmd.clone.sunk | while | flops 199746 | bytes 232601 | solution.py:62
  245.2 1.1 constant_dynamic-slice_fusion.9
  247.5 1.2 constant_dynamic-slice_fusion.9
  276.3 2.5 fusion.53
  279.8 3.8 %fusion.50 = f32[8,16,16,16]{3,1,2,0:T(8,128)S(1)} fusion(f32[8,16,16,16]{3,1,2,0:T(8,128)S(1)} %fusion.51, f32[8,16,16,128]{3,2,1,0:T(8,128)S(1)} %get-tuple-element.490, f32[8,16,16]{1,2,0:T(8,128)S(1)} %copy-done.8, bf16[16,8,128]{2,1,0:T(8,128)(2,1)S(1)} %copy-done.12), kind=kOutput, calls=%fused_computation.78 | convolution fusion | flops 50397184 | bytes 1351680 | tf_op jit(solution)/shard_map/lks,lhps->lkhp/dot_general | solution.py:159
  285.1 6.3 %while.131 = (s32[]{:T(128)}, f32[8,16,16,128]{3,2,1,0:T(8,128)S(1)}, s32[]{:T(128)}, bf16[4,8,16]{2,1,0:T(8,128)(2,1)}, bf16[4,8,16,16,128]{4,3,2,1,0:T(8,128)(...) while((s32[]{:T(128)}, f32[8,16,16,128]{3,2,1,0:T(8,128)S(1)}, s32[]{:T(128)}, ...), condition=%wide.region_20.21_spmd, body=%wide.region_19.20_spmd.sunk | while | flops 786566 | bytes 2622875 | solution.py:46
  286.0 1.3 convert_add_fusion.12
  288.0 1.3 convert_add_fusion.12
  290.1 1.3 convert_add_fusion.12
  291.4 3.8 %fusion.48 = f32[8,16,16,16]{3,1,2,0:T(8,128)S(1)} fusion(f32[8,16,16,16]{3,1,2,0:T(8,128)S(1)} %fusion.49, f32[8,16,16,128]{3,2,1,0:T(8,128)S(1)} %get-tuple-element.492, f32[8,16,16]{1,2,0:T(8,128)S(1)} %copy-done.6, bf16[8,16,128]{2,1,0:T(8,128)(2,1)S(1)} %copy-done.10), kind=kOutput, calls=%fused_computation.73 | convolution fusion | flops 50397184 | bytes 1351680 | tf_op jit(solution)/shard_map/lks,lhps->lkhp/dot_general | solution.py:159
  296.9 1.2 copy-done.2
  298.0 8.2 %fusion.54 = f32[16,8,16,16]{3,1,2,0:T(8,128)S(1)} fusion(f32[16,8,16,16]{3,1,2,0:T(8,128)S(1)} %copy-done.2, f32[16,16,16,128]{3,2,1,0:T(8,128)S(1)} %get-tuple-element.486, f32[16,8,16]{1,2,0:T(8,128)S(1)} %copy-done.4, bf16[16,8,256]{2,1,0:T(8,128)(2,1)} %copy-done.5), kind=kOutput, calls=%fused_computation.87 | convolution fusion | flops 50397184 | bytes 2400256 | tf_op jit(solution)/shard_map/lks,lhps->lkhp/dot_general | solution.py:159
  307.5 13.9 %all-gather.17.cloned.1.call-done = bf16[128,16,16,128]{3,2,1,0:T(8,128)(2,1)} async-done(((bf16[16,16,16,128]{3,2,1,0:T(8,128)(2,1)}), bf16[128,16,16,128]{3,2,1,0:T(8,128)(2,1)}) %all-gather.17.cloned.1.call-update) | async-done | bytes 8388624 | tf_op jit(solution)/shard_map/all_gather | solution.py:31
  321.6 17.5 %while.129 = (s32[]{:T(128)}, f32[16,16,16,128]{3,2,1,0:T(8,128)S(1)}, s32[]{:T(128)}, bf16[8,16,16]{2,1,0:T(8,128)(2,1)}, bf16[8,16,16,16,128]{4,3,2,1,0:T(8,12...) while((s32[]{:T(128)}, f32[16,16,16,128]{3,2,1,0:T(8,128)S(1)}, s32[]{:T(128)}, ...), condition=%wide.region_10.11_spmd, body=%wide.region_9.10_spmd.sunk | while | flops 1573126 | bytes 5245595 | solution.py:46
  322.4 1.7 convert_add_fusion.10
  324.9 1.7 convert_add_fusion.10
  327.3 1.7 convert_add_fusion.10
  329.8 1.7 convert_add_fusion.10
  332.2 1.7 convert_add_fusion.10
  334.7 1.7 convert_add_fusion.10
  337.1 1.7 convert_add_fusion.10
  339.2 8.2 %fusion.52 = f32[16,8,16,16]{3,1,2,0:T(8,128)S(1)} fusion(f32[16,8,16,16]{3,1,2,0:T(8,128)S(1)} %copy-done.1, f32[16,16,16,128]{3,2,1,0:T(8,128)S(1)} %get-tuple-element.488, f32[16,8,16]{1,2,0:T(8,128)S(1)} %copy-done.3, bf16[16,8,128]{2,1,0:T(8,128)(2,1)} %rev.45), kind=kOutput, calls=%fused_computation.83 | convolution fusion | flops 50397184 | bytes 2400256 | tf_op jit(solution)/shard_map/lks,lhps->lkhp/dot_general | solution.py:159
  (444 shorter events, 136.3 us)
Async XLA Ops:
  6.5 46.3 %copy-start = (bf16[256,512]{1,0:T(8,128)(2,1)S(1)}, bf16[256,512]{1,0:T(8,128)(2,1)}, u32[]{:S(2)}) copy-start(bf16[256,512]{1,0:T(8,128)(2,1)} %param.36) | copy-start | bytes 786436
  6.5 61.1 %copy-start.23 = (bf16[256,64]{0,1:T(8,128)(2,1)S(1)}, bf16[256,64]{0,1:T(8,128)(2,1)}, u32[]{:S(2)}) copy-start(bf16[256,64]{0,1:T(8,128)(2,1)} %param.39) | copy-start | bytes 98308
  6.5 61.3 %copy-start.22 = (f32[16,8]{0,1:T(8,128)S(1)}, f32[16,8]{0,1:T(8,128)}, u32[]{:S(2)}) copy-start(f32[16,8]{0,1:T(8,128)} %param.43) | copy-start | bytes 1540
  6.5 272.3 %all-gather.19.cloned.1.call-start = ((), (), s32[]{:S(2)}) async-start(), calls=%async_computation.2 | async-start | bytes 2621440 | tf_op jit(solution)/shard_map/all_gather | solution.py:31
  51.8 10.4 %copy-start.20 = (f32[8,256]{1,0:T(8,128)}, f32[8,256]{1,0:T(8,128)S(1)}, u32[]{:S(2)}) copy-start(f32[8,256]{1,0:T(8,128)S(1)} %fusion.149) | copy-start | bytes 24580
  53.9 8.3 %copy-start.16 = (bf16[16,8,512]{2,1,0:T(8,128)(2,1)}, bf16[16,8,512]{2,1,0:T(8,128)(2,1)S(1)}, u32[]{:S(2)}) copy-start(bf16[16,8,512]{2,1,0:T(8,128)(2,1)S(1)} %fusion.60) | copy-start | bytes 393220
  53.9 8.3 %collective-permute-start.1 = (bf16[1,8,256]{2,1,0:T(8,128)(2,1)S(1)}, bf16[1,8,256]{2,1,0:T(8,128)(2,1)S(1)}, u32[]{:S(2)}, u32[]{:S(2)}) collective-permute-start(bf16[1,8,256]{2,1,0:T(8,128)(2,1)S(1)} %get-tuple-element.727), channel_id=1, source_target_pairs={{8,0},{16,8},{24,16},{9,1},{17,9},{25,17},{10,2},{18,10},{26,18},{... | collective-permute-start | bytes 12296 | tf_op jit(solution)/shard_map/ppermute | solution.py:19
  55.2 7.0 %collective-permute-start = (bf16[1,8,256]{2,1,0:T(8,128)(2,1)S(1)}, bf16[1,8,256]{2,1,0:T(8,128)(2,1)S(1)}, u32[]{:S(2)}, u32[]{:S(2)}) collective-permute-start(bf16[1,8,256]{2,1,0:T(8,128)(2,1)S(1)} %get-tuple-element.726), channel_id=1, source_target_pairs={{0,8},{8,16},{16,24},{1,9},{9,17},{17,25},{2,10},{10,18},{18,26},{... | collective-permute-start | bytes 12296 | tf_op jit(solution)/shard_map/ppermute | solution.py:17
  62.2 3.7 %collective-permute-start.2 = (bf16[18,1,256]{2,1,0:T(2,128)(2,1)S(1)}, bf16[18,1,256]{2,1,0:T(2,128)(2,1)S(1)}, u32[]{:S(2)}, u32[]{:S(2)}) collective-permute-start(bf16[18,1,256]{2,1,0:T(2,128)(2,1)S(1)} %get-tuple-element.730), channel_id=1, source_target_pairs={{0,1},{1,2},{2,3},{3,4},{4,5},{5,6},{6,7},{8,9},{9,10},{10,11},{11... | collective-permute-start | bytes 27656 | tf_op jit(solution)/shard_map/ppermute | solution.py:17
  63.9 3.1 collective-permute-start.3
  70.1 0.6 copy-start.11
  77.6 70.7 %copy-start.7 = (f32[8,16,16]{1,2,0:T(8,128)}, f32[8,16,16]{1,2,0:T(8,128)S(1)}, u32[]{:S(2)}) copy-start(f32[8,16,16]{1,2,0:T(8,128)S(1)} %copy.193) | copy-start | bytes 24580
  80.6 3.7 %copy-start.24 = (bf16[256,64]{0,1:T(8,128)(2,1)S(1)}, bf16[256,64]{0,1:T(8,128)(2,1)}, u32[]{:S(2)}) copy-start(bf16[256,64]{0,1:T(8,128)(2,1)} %param.39) | copy-start | bytes 98308
  80.6 5.3 %copy-start.25 = (f32[16]{0:T(128)S(1)}, f32[16]{0:T(128)}, u32[]{:S(2)}) copy-start(f32[16]{0:T(128)} %get-tuple-element.782) | copy-start | bytes 196
  80.6 204.4 %all-gather.21.cloned.1.call-start = ((), (), s32[]{:S(2)}) async-start(), calls=%async_computation.3 | async-start | bytes 2621440 | tf_op jit(solution)/shard_map/all_gather | solution.py:31
  83.3 58.9 %copy-start.9 = (bf16[8,16,128]{2,1,0:T(8,128)(2,1)}, bf16[8,16,128]{2,1,0:T(8,128)(2,1)S(1)}, u32[]{:S(2)}) copy-start(bf16[8,16,128]{2,1,0:T(8,128)(2,1)S(1)} %rev.51) | copy-start | bytes 98308
  90.1 53.1 %copy-start.18 = (f32[16,8,16]{2,1,0:T(8,128)S(1)}, f32[16,8,16]{2,1,0:T(8,128)}, u32[]{:S(2)}) copy-start(f32[16,8,16]{2,1,0:T(8,128)} %copy.166) | copy-start | bytes 24580
  90.1 206.5 %all-gather.15.cloned.1.call-start = ((), (), s32[]{:S(2)}) async-start(), calls=%async_computation | async-start | bytes 9437184 | tf_op jit(solution)/shard_map/all_gather | solution.py:31
  142.2 3.1 copy-start.5
  149.5 171.8 %all-gather.17.cloned.1.call-start = ((), (), s32[]{:S(2)}) async-start(), calls=%async_computation.1 | async-start | bytes 9437184 | tf_op jit(solution)/shard_map/all_gather | solution.py:31
  278.9 0.8 copy-start.8
  278.9 0.8 copy-start.12
  285.1 6.4 %copy-start.6 = (f32[8,16,16]{1,2,0:T(8,128)S(1)}, f32[8,16,16]{1,2,0:T(8,128)}, u32[]{:S(2)}) copy-start(f32[8,16,16]{1,2,0:T(8,128)} %copy.205) | copy-start | bytes 24580
  285.1 6.4 %copy-start.10 = (bf16[8,16,128]{2,1,0:T(8,128)(2,1)S(1)}, bf16[8,16,128]{2,1,0:T(8,128)(2,1)}, u32[]{:S(2)}) copy-start(bf16[8,16,128]{2,1,0:T(8,128)(2,1)} %copy-done.9) | copy-start | bytes 98308
  296.8 1.2 copy-start.2
  296.8 1.2 copy-start.4
  321.6 17.6 %copy-start.1 = (f32[16,8,16,16]{3,1,2,0:T(8,128)S(1)}, f32[16,8,16,16]{3,1,2,0:T(8,128)}, u32[]{:S(2)}) copy-start(f32[16,8,16,16]{3,1,2,0:T(8,128)} %fusion.53) | copy-start | bytes 393220
  321.6 17.6 %copy-start.3 = (f32[16,8,16]{1,2,0:T(8,128)S(1)}, f32[16,8,16]{1,2,0:T(8,128)}, u32[]{:S(2)}) copy-start(f32[16,8,16]{1,2,0:T(8,128)} %copy.181) | copy-start | bytes 24580
  347.4 0.9 copy-start.13
  347.4 1.0 copy-start.14
  347.4 1.0 copy-start.15
  347.4 1.1 copy-start.17
  347.4 1.1 copy-start.19
  347.4 1.1 copy-start.21
  347.4 1.2 copy-start.26
  347.4 1.2 copy-start.27
Sparse Core Ops, SparseCore 0:
  80.7 33.7 all-gather.18
  116.3 35.2 all-gather.20
  153.3 82.0 all-gather.14
  240.8 80.5 all-gather.16
where the time goes:
time: 362 us; the launch traced here: 356 us
  local copies, waits for them, and re-layouts  106 us (29%)
  blocking collectives  89.5 us (25%)
  matrix products  85.6 us (24%)
  other arithmetic  33.6 us (9%)
  waiting for transfers between devices  15 us (4%)
  between operations  14 us (4%)
  starting transfers between devices  8.92 us (2%)
    dynamic_slice x64, local copies, waits for them, and re-layouts, segment_recurrence(): lax.map(head_term, (jnp.moveaxis(cumulative, 2, 0), jnp.moveaxis(driven,...  54 us
    all_gather x4, blocking collectives, entering(): lax.all_gather(a.astype(kind), axis)  46.2 us
    all_gather x1, blocking collectives, per_device(): lax.all_gather(local_tokens, ('row', 'col'), axis=0, tiled=True)  43.3 us
    sub x96, local copies, waits for them, and re-layouts, head_term(): head_cum[:, :, None] - head_cum[:, None, :]  35.4 us
    dot_general x64, matrix products, head_term(): jnp.einsum('lkj,ljp->lkp', scores * jnp.exp(spread), head_drive, precisio...  32.1 us
    dot_general x4, matrix products, finish(): jnp.einsum('lks,lhps->lkhp', out_l.astype(jnp.float32), inflow, precision...  23.9 us
    add x10, other arithmetic, combine_states(): later[0][:, :, None, None] * earlier[1] + later[1]  16.2 us
    all_gather x4, waiting for transfers between devices, entering(): lax.all_gather(a.astype(kind), axis)  13.9 us
  transfers between devices with their start and end apart: 8, of which 2 were waited for; matrix products, arithmetic and copies ran while one was open for 50% of the time, Pallas kernels for 0%

commit v1 on v0

v1 whole, which is shorter than its diff:
```python
import functools

import jax
import jax.numpy as jnp
from jax import lax
from jax.experimental import pallas as pl
from jax.experimental.pallas import tpu as pltpu
from jax.sharding import PartitionSpec as P

MESH = pl.DeviceIdType.MESH
F32 = jnp.float32
BF16 = jnp.bfloat16


def exact_dot(a, b):
    return jnp.dot(a, b, preferred_element_type=F32, precision=lax.Precision.HIGHEST)


def dot(a, b):
    return jnp.dot(a.astype(BF16), b.astype(BF16), preferred_element_type=F32)


def dot_t(a, b):
    return lax.dot_general(
        a.astype(BF16), b.astype(BF16), (((1,), (1,)), ((), ())), preferred_element_type=F32
    )


def silu(v):
    return v / (1.0 + jnp.exp(-v))


def softplus(v):
    return jnp.maximum(v, 0.0) + jnp.log1p(jnp.exp(-jnp.abs(v)))


def kernel(
    n_row,
    n_col,
    latent_ref,
    logs_ref,
    cond_ref,
    trace_ref,
    norm_gain_ref,
    in_ref,
    conv_ref,
    bc_ref,
    dt_ref,
    dt_bias_ref,
    row_rate_ref,
    col_rate_ref,
    horizon_ref,
    out_gain_ref,
    out_weight_ref,
    out_ref,
    lat_f,
    logs_f,
    logs_all,
    logs_flat,
    picks,
    picks_side,
    edge_out,
    edge_line,
    edge_side,
    hz_row,
    hz_col,
    strip_row,
    strip_col,
    logs_send,
    logs_recv,
    edge_send,
    edge_recv,
    hz_send_r,
    hz_recv_r,
    hz_send_c,
    hz_recv_c,
    mix_send_r,
    mix_recv_r,
    mix_send_c,
    mix_recv_c,
):
    rows, cols, width = latent_ref.shape
    cells = rows * cols
    count = n_row * n_col
    inner = in_ref.shape[1] // 2
    heads = dt_bias_ref.shape[1]
    head_dim = inner // heads
    state = bc_ref.shape[1] // 8
    lanes = 4 * heads
    r = lax.axis_index("row")
    c = lax.axis_index("col")
    me = r * n_col + c
    n_token = logs_all.shape[0] * logs_all.shape[1]
    up, down = lax.rem(r + n_row - 1, n_row), lax.rem(r + 1, n_row)
    left, right = lax.rem(c + n_col - 1, n_col), lax.rem(c + 1, n_col)

    barrier = pltpu.get_barrier_semaphore()

    def greet(o, carry):
        d = lax.rem(me + o, count)
        pl.semaphore_signal(
            barrier, inc=1, device_id=(d // n_col, lax.rem(d, n_col)), device_id_type=MESH
        )
        return carry

    lax.fori_loop(1, count, greet, 0)

    lat = latent_ref[...].astype(F32)
    lat_f[...] = lat
    edge_out[0] = lat_f[:, 0, :]
    edge_out[1] = lat_f[:, cols - 1, :]
    logs_f[...] = logs_ref[...].astype(F32)
    logs_all[me] = logs_f[...]
    sub = lax.broadcasted_iota(jnp.int32, (cols, n_token), 0)
    lane = lax.broadcasted_iota(jnp.int32, (cols, n_token), 1)
    want = jnp.zeros((cols, n_token), jnp.int32)
    for j in range(cols):
        want = jnp.where(sub == j, trace_ref[j], want)
    picks[...] = (want == lane).astype(F32)
    hz_row[c] = horizon_ref[...]
    hz_col[r] = horizon_ref[...]

    pl.semaphore_wait(barrier, count - 1)

    def logs_copy(o):
        d = lax.rem(me + o, count)
        return pltpu.make_async_remote_copy(
            src_ref=logs_f,
            dst_ref=logs_all.at[me],
            send_sem=logs_send.at[o],
            recv_sem=logs_recv.at[o],
            device_id=(d // n_col, lax.rem(d, n_col)),
            device_id_type=MESH,
        )

    def start_logs(o, carry):
        logs_copy(o).start()
        return carry

    lax.fori_loop(1, count, start_logs, 0)

    last = rows - 1
    edges = []
    for src, dst, to in (
        (picks, picks_side.at[0], (r, right)),
        (picks, picks_side.at[1], (r, left)),
        (edge_out.at[1], edge_side.at[0], (r, right)),
        (edge_out.at[0], edge_side.at[1], (r, left)),
        (lat_f.at[last], edge_line.at[0], (down, c)),
        (lat_f.at[last], edge_line.at[1], (down, right)),
        (lat_f.at[last], edge_line.at[2], (down, left)),
        (lat_f.at[0], edge_line.at[3], (up, c)),
        (lat_f.at[0], edge_line.at[4], (up, right)),
        (lat_f.at[0], edge_line.at[5], (up, left)),
    ):
        k = len(edges)
        edges.append(
            pltpu.make_async_remote_copy(
                src_ref=src,
                dst_ref=dst,
                send_sem=edge_send.at[k],
                recv_sem=edge_recv.at[k],
                device_id=to,
                device_id_type=MESH,
            )
        )
        edges[-1].start()

    def fan(buffer_r, buffer_c, send_r, recv_r, send_c, recv_c):
        copies = []
        for o in range(1, n_col):
            copies.append(
                pltpu.make_async_remote_copy(
                    src_ref=buffer_r.at[c],
                    dst_ref=buffer_r.at[c],
                    send_sem=send_r.at[o],
                    recv_sem=recv_r.at[o],
                    device_id=(r, lax.rem(c + o, n_col)),
                    device_id_type=MESH,
                )
            )
        for o in range(1, n_row):
            copies.append(
                pltpu.make_async_remote_copy(
                    src_ref=buffer_c.at[r],
                    dst_ref=buffer_c.at[r],
                    send_sem=send_c.at[o],
                    recv_sem=recv_c.at[o],
                    device_id=(lax.rem(r + o, n_row), c),
                    device_id_type=MESH,
                )
            )
        for copy in copies:
            copy.start()
        return copies

    hz_copies = fan(hz_row, hz_col, hz_send_r, hz_recv_r, hz_send_c, hz_recv_c)

    head_of = lax.broadcasted_iota(jnp.int32, (heads, lanes), 1)
    spread = (
        lax.rem(head_of, heads) == lax.broadcasted_iota(jnp.int32, (heads, lanes), 0)
    ).astype(F32)

    def lane_row(table, first):
        wide = exact_dot(table, spread)
        kind = lax.broadcasted_iota(jnp.int32, wide.shape, 1) // heads
        own = lax.broadcasted_iota(jnp.int32, wide.shape, 0) + first
        return jnp.sum(jnp.where(kind == own, wide, 0.0), axis=0, keepdims=True)

    bias = lane_row(dt_bias_ref[...], 0)
    rates = lane_row(row_rate_ref[...] / (16.0 * cols * n_col), 0) + lane_row(
        col_rate_ref[...] / (16.0 * rows * n_row), 2
    )
    lane_dir = lax.broadcasted_iota(jnp.int32, (cells, lanes), 1) // heads
    ex_lane = lax.broadcasted_iota(jnp.int32, (lanes, inner), 0)
    ex_head = lax.broadcasted_iota(jnp.int32, (lanes, inner), 1) // head_dim
    expand = [(ex_lane == ex_head + k * heads).astype(BF16) for k in range(4)]

    cell_t = lax.broadcasted_iota(jnp.int32, (cells, cells), 0)
    cell_s = lax.broadcasted_iota(jnp.int32, (cells, cells), 1)
    ti, tj = cell_t // cols, lax.rem(cell_t, cols)
    si, sj = cell_s // cols, lax.rem(cell_s, cols)

    n_src = cells + 6 * cols + 2 * rows
    src_id = lax.broadcasted_iota(jnp.int32, (cells, n_src), 1)
    cell_id = lax.broadcasted_iota(jnp.int32, (cells, 1), 0)
    ci, cj = cell_id // cols, lax.rem(cell_id, cols)
    shifts = []
    for a in range(3):
        for b in range(3):
            pi, pj = ci + a - 1, cj + b - 1
            row_in = (pi >= 0) & (pi < rows)
            where_from = pi * cols + pj
            line_base = jnp.where(pi < 0, cells, cells + 3 * cols)
            line_from = line_base + jnp.where(
                pj < 0, 2 * cols - 1, jnp.where(pj >= cols, 2 * cols, pj)
            )
            side_from = cells + 6 * cols + pi + jnp.where(pj < 0, 0, rows)
            source = jnp.where(
                row_in, jnp.where((pj >= 0) & (pj < cols), where_from, side_from), line_from
            )
            gi, gj = r * rows + pi, c * cols + pj
            inside = (gi >= 0) & (gi < n_row * rows) & (gj >= 0) & (gj < n_col * cols)
            source = jnp.where(inside, source, -1)
            shifts.append((src_id == source).astype(BF16))

    def wait_logs(o, carry):
        logs_copy(o).wait()
        return carry

    lax.fori_loop(1, count, wait_logs, 0)
    per = logs_all.shape[1]
    for k in range(logs_all.shape[0]):
        logs_flat[pl.ds(k * per, per), :] = logs_all[k]
    tokens = silu(dot(logs_flat[...], cond_ref[...])).astype(BF16)

    for edge in edges:
        edge.wait()
    own_tokens = dot(picks[...], tokens)
    left_tokens = dot(picks_side[0], tokens)
    right_tokens = dot(picks_side[1], tokens)

    hidden_own = (lat_f[...] + own_tokens[None]).reshape(cells, width)
    left_token = left_tokens[cols - 1 : cols]
    right_token = right_tokens[0:1]
    hidden = jnp.concatenate(
        [
            hidden_own,
            edge_line[0] + own_tokens,
            edge_line[1] + left_tokens,
            edge_line[2] + right_tokens,
            edge_line[3] + own_tokens,
            edge_line[4] + left_tokens,
            edge_line[5] + right_tokens,
            edge_side[0] + left_token,
            edge_side[1] + right_token,
        ],
        axis=0,
    )
    normed = (
        hidden
        * lax.rsqrt(jnp.mean(hidden * hidden, axis=-1, keepdims=True) + 1e-06)
        * norm_gain_ref[...]
    ).astype(BF16)
    pre_conv = dot(normed, in_ref[:, :inner]).astype(BF16)
    gate_part = dot(normed[:cells], in_ref[:, inner:]).astype(BF16)
    conv_sum = jnp.zeros((cells, inner), F32)
    for k in range(9):
        conv_sum = conv_sum + dot(shifts[k], pre_conv) * conv_ref[k : k + 1, :]
    mixed = silu(conv_sum).astype(BF16)
    strip_row[c] = mixed
    strip_col[r] = mixed
    mix_copies = fan(strip_row, strip_col, mix_send_r, mix_recv_r, mix_send_c, mix_recv_c)

    mixed_f = mixed.astype(F32)
    coefs = dot(mixed, bc_ref[...]).astype(BF16)
    in_coef = [coefs[:, 2 * k * state : (2 * k + 1) * state] for k in range(4)]
    out_coef = [coefs[:, (2 * k + 1) * state : (2 * k + 2) * state] for k in range(4)]

    def spread_horizon(tile):
        pick = (
            lax.broadcasted_iota(jnp.int32, (cells, rows), 0) // cols
            == lax.broadcasted_iota(jnp.int32, (cells, rows), 1)
        ).astype(F32)
        wide = exact_dot(pick, tile)
        column = lax.rem(lax.broadcasted_iota(jnp.int32, (cells, cols), 0), cols)
        keep = column == lax.broadcasted_iota(jnp.int32, (cells, cols), 1)
        return jnp.sum(jnp.where(keep, wide, 0.0), axis=1, keepdims=True)

    def steps_of(x, marks):
        step = softplus(dot(x, dt_ref[...]) + bias)
        return step, -step * rates - marks

    step, decay = steps_of(mixed, spread_horizon(horizon_ref[...]))
    total = jnp.zeros((cells, inner), F32)
    entry = []
    for k in range(4):
        if k < 2:
            same, pt, ps, length = ti == si, tj, sj, cols
        else:
            same, pt, ps, length = tj == sj, ti, si, rows
        if k % 2 == 1:
            pt, ps = length - 1 - pt, length - 1 - ps
        scores = dot_t(out_coef[k], in_coef[k])
        total = total + dot(
            jnp.where(cell_t == cell_s, scores, 0.0), mixed_f * dot(step, expand[k])
        )
        half = length // 2
        while half >= 1:
            bt, bs = pt // half, ps // half
            late = lax.rem(bt, 2) == 1
            reach = same & (bt == bs) & ((late & (ps <= pt)) | (~late & (ps > pt)))
            factor = jnp.exp(exact_dot(reach.astype(F32), decay))
            pair = same & (bt == bs + 1) & late
            total = total + dot(factor, expand[k]) * dot(
                jnp.where(pair, scores, 0.0), mixed_f * dot(factor * step, expand[k])
            )
            half //= 2
        reach = (same & (ps <= pt)).astype(F32)
        entry.append(dot(jnp.exp(exact_dot(reach, decay)), expand[k]))

    for copy in hz_copies:
        copy.wait()
    marks_row = [spread_horizon(hz_row[q]) for q in range(n_col)]
    marks_col = [spread_horizon(hz_col[q]) for q in range(n_row)]
    for copy in mix_copies:
        copy.wait()

    for first, strip, marks, place, n, same, later in (
        (0, strip_row, marks_row, c, n_col, ti == si, sj - tj),
        (2, strip_col, marks_col, r, n_row, tj == sj, si - ti),
    ):
        after = (same & (later > 0)).astype(F32)
        before = (same & (later < 0)).astype(F32)
        whole = same.astype(F32)
        xs, steps, sums_f, sums_b, totals = [], [], [], [], []
        for q in range(n):
            x = strip[q]
            step, decay = steps_of(x, marks[q])
            xs.append(x)
            steps.append(step)
            sums_f.append(exact_dot(after, decay))
            sums_b.append(exact_dot(before, decay))
            totals.append(exact_dot(whole, decay))
        carry = jnp.zeros((cells, lanes), F32)
        for q in reversed(range(n)):
            sums_f[q] = sums_f[q] + carry
            carry = carry + jnp.where(q < place, totals[q], 0.0)
        carry = jnp.zeros((cells, lanes), F32)
        for q in range(n):
            sums_b[q] = sums_b[q] + carry
            carry = carry + jnp.where(q > place, totals[q], 0.0)
        both = expand[first] + expand[first + 1]
        weight_f = bc_ref[:, 2 * first * state : (2 * first + 1) * state]
        weight_b = bc_ref[:, (2 * first + 2) * state : (2 * first + 3) * state]
        for q in range(n):
            ahead = q < place
            use = ((lane_dir == first) & ahead) | ((lane_dir == first + 1) & (q > place))
            sums = jnp.where(lane_dir == first, sums_f[q], sums_b[q])
            gain = jnp.where(use, steps[q] * jnp.exp(sums), 0.0)
            driven = xs[q].astype(F32) * dot(gain, both)
            coef = dot(xs[q], jnp.where(ahead, weight_f, weight_b))
            reader = jnp.where(ahead, out_coef[first], out_coef[first + 1])
            scores = jnp.where(same, dot_t(reader, coef), 0.0)
            total = total + jnp.where(ahead, entry[first], entry[first + 1]) * dot(scores, driven)

    gated = (
        total
        * lax.rsqrt(jnp.mean(total * total, axis=-1, keepdims=True) + 1e-05)
        * out_gain_ref[...]
        * silu(gate_part.astype(F32))
    ).astype(BF16)
    result = hidden_own + dot(gated, out_weight_ref[...])
    out_ref[...] = result.reshape(rows, cols, width).astype(BF16)


def per_device(n_row, n_col, *args):
    (
        latent,
        logs,
        cond,
        trace,
        norm_gain,
        in_weight,
        conv,
        bc,
        dt,
        dt_bias,
        row_rate,
        col_rate,
        horizon,
        out_gain,
        out_weight,
    ) = args
    rows, cols, width = latent.shape
    inner = in_weight.shape[1] // 2
    cells = rows * cols
    count = n_row * n_col
    per = logs.shape[0]
    vmem = pl.BlockSpec(memory_space=pltpu.VMEM)
    specs = [vmem] * 15
    specs[3] = pl.BlockSpec(memory_space=pltpu.SMEM)
    dma = pltpu.SemaphoreType.DMA
    return pl.pallas_call(
        functools.partial(kernel, n_row, n_col),
        out_shape=jax.ShapeDtypeStruct((rows, cols, width), BF16),
        in_specs=specs,
        out_specs=vmem,
        scratch_shapes=[
            pltpu.VMEM((rows, cols, width), F32),
            pltpu.VMEM((per, width), F32),
            pltpu.VMEM((count, per, width), F32),
            pltpu.VMEM((count * per, width), F32),
            pltpu.VMEM((cols, count * per), F32),
            pltpu.VMEM((2, cols, count * per), F32),
            pltpu.VMEM((2, rows, width), F32),
            pltpu.VMEM((6, cols, width), F32),
            pltpu.VMEM((2, rows, width), F32),
            pltpu.VMEM((n_col, rows, cols), F32),
            pltpu.VMEM((n_row, rows, cols), F32),
            pltpu.VMEM((n_col, cells, inner), BF16),
            pltpu.VMEM((n_row, cells, inner), BF16),
            dma((count,)),
            dma((count,)),
            dma((10,)),
            dma((10,)),
            dma((n_col,)),
            dma((n_col,)),
            dma((n_row,)),
            dma((n_row,)),
            dma((n_col,)),
            dma((n_col,)),
            dma((n_row,)),
            dma((n_row,)),
        ],
        compiler_params=pltpu.CompilerParams(
            collective_id=0, has_side_effects=True, vmem_limit_bytes=48 * 1024 * 1024
        ),
    )(
        latent,
        logs,
        cond,
        trace,
        norm_gain.reshape(1, width),
        in_weight,
        conv,
        bc,
        dt,
        dt_bias,
        row_rate,
        col_rate,
        horizon,
        out_gain.reshape(1, inner),
        out_weight,
    )


def solution(mesh):
    placed = (
        P("row", "col", None),
        P(("row", "col"), None),
        P(),
        P("col"),
        P(),
        P(),
        P(),
        P(),
        P(),
        P(),
        P(),
        P(),
        P("row", "col"),
        P(),
        P(),
    )
    return jax.shard_map(
        functools.partial(per_device, mesh.shape["row"], mesh.shape["col"]),
        mesh=mesh,
        in_specs=placed,
        out_specs=P("row", "col", None),
        check_vma=False,
    )
```

time: 362 us -> 38.6 us (0.11)
  the two profiles are of different devices: /device:TPU:0 before, /device:TPU:9 now
where the time goes in v1:
time: 38.6 us; the launch traced here: 38.2 us
  Pallas kernels  31.9 us (83%)
  local copies, waits for them, and re-layouts  6.19 us (16%)
    pallas_call x1, Pallas kernels, per_device(): pl.pallas_call(functools.partial(kernel, n_row, n_col), out_shape=jax.Sha...  31.9 us
    unnamed x29, local copies, waits for them, and re-layouts  6.19 us

profile of v1, /device:TPU:9, one launch (start us, length us, event | category | flops | bytes accessed | tf_op | source)
XLA Modules:
  0.0 38.2 jit_solution(9887823931037807027)
XLA Ops:
  0.0 0.0 copy-start.4
  0.0 0.8 %copy.17.horizon_ref = f32[16,8]{1,0:T(8,128)S(1)} copy(f32[16,8]{0,1:T(8,128)} %param.27) | data formatting | bytes 1024 | tf_op args[12]
  0.8 0.0 copy-start.5
  0.8 0.0 copy-start.6
  0.8 0.0 copy-start.7
  0.8 0.0 copy-start.8
  0.8 0.0 copy-start.9
  0.8 0.0 copy-start.10
  0.8 0.0 copy-start.11
  0.8 0.0 copy-start.12
  0.9 0.9 %copy.16.dt_ref = bf16[256,64]{1,0:T(8,128)(2,1)S(1)} copy(bf16[256,64]{0,1:T(8,128)(2,1)} %param.23) | data formatting | bytes 65536 | tf_op args[8]
  1.8 0.0 copy-done.4
  1.8 0.0 copy-done.5
  1.8 0.0 copy-done.6
  1.8 0.0 copy-done.7
  1.8 0.0 copy-done.8
  1.8 0.0 copy-done.9
  1.9 0.0 copy-done.10
  1.9 0.0 copy-done.11
  1.9 0.0 copy-done.12
  1.9 0.0 copy-start
  1.9 1.0 %copy-done = bf16[256,1024]{1,0:T(8,128)(2,1)S(1)} copy-done((bf16[256,1024]{1,0:T(8,128)(2,1)S(1)}, bf16[256,1024]{1,0:T(8,128)(2,1)}, u32[]{:S(2)}) %copy-start) | copy-done | bytes 524312
  2.9 0.0 copy-start.1
  2.9 0.9 %copy-done.1 = bf16[256,512]{1,0:T(8,128)(2,1)S(1)} copy-done((bf16[256,512]{1,0:T(8,128)(2,1)S(1)}, bf16[256,512]{1,0:T(8,128)(2,1)}, u32[]{:S(2)}) %copy-start.1) | copy-done | bytes 262168
  3.9 0.0 copy-start.2
  3.9 0.9 %copy-done.2 = bf16[256,256]{1,0:T(8,128)(2,1)S(1)} copy-done((bf16[256,256]{1,0:T(8,128)(2,1)S(1)}, bf16[256,256]{1,0:T(8,128)(2,1)}, u32[]{:S(2)}) %copy-start.2) | copy-done | bytes 131096
  4.8 0.0 copy-start.3
  4.8 0.9 %copy-done.3 = bf16[256,256]{1,0:T(8,128)(2,1)S(1)} copy-done((bf16[256,256]{1,0:T(8,128)(2,1)S(1)}, bf16[256,256]{1,0:T(8,128)(2,1)}, u32[]{:S(2)}) %copy-start.3) | copy-done | bytes 131096
  5.7 31.9 %shard_map.145 = bf16[16,8,256]{2,1,0:T(8,128)(2,1)S(1)} custom-call(bf16[16,8,256]{2,1,0:T(8,128)(2,1)S(1)} %copy-done.4, bf16[1,256]{1,0:T(2,128)(2,1)S(1)} %copy-done.7, bf16[256,256]{1,0:T(8,128)(2,1)S(1)} %copy-done.2, s32[8]{0:T(128)S(1)} %copy-done.12, f32[1,256]{1,0:T(1,128)S(1)} %bitcast.2, bf16[256,512]{1,0:T(8,128)(2,1)S(1)} %copy-done.1, ...), custom_call_target="tpu_custom_call" | custom-call | tf_op jit(solution)/shard_map/pallas_call | solution.py:424
  37.6 0.6 %copy.19 = bf16[16,8,256]{2,1,0:T(8,128)(2,1)} copy(bf16[16,8,256]{2,1,0:T(8,128)(2,1)S(1)} %shard_map.145) | data formatting | bytes 131072
Async XLA Ops:
  0.0 1.8 %copy-start.4 = (bf16[16,8,256]{2,1,0:T(8,128)(2,1)S(1)}, bf16[16,8,256]{2,1,0:T(8,128)(2,1)}, u32[]{:S(2)}) copy-start(bf16[16,8,256]{2,1,0:T(8,128)(2,1)} %latent_ref.1) | copy-start | bytes 196612
  0.8 1.0 %copy-start.5 = (f32[9,256]{1,0:T(8,128)S(1)}, f32[9,256]{1,0:T(8,128)}, u32[]{:S(2)}) copy-start(f32[9,256]{1,0:T(8,128)} %conv_ref.1) | copy-start | bytes 27652
  0.8 1.0 %copy-start.6 = (f32[4,16]{1,0:T(4,128)S(1)}, f32[4,16]{1,0:T(4,128)}, u32[]{:S(2)}) copy-start(f32[4,16]{1,0:T(4,128)} %dt_bias_ref.1) | copy-start | bytes 772
  0.8 1.0 %copy-start.7 = (bf16[1,256]{1,0:T(2,128)(2,1)S(1)}, bf16[1,256]{1,0:T(2,128)(2,1)}, u32[]{:S(2)}) copy-start(bf16[1,256]{1,0:T(2,128)(2,1)} %logs_ref.1) | copy-start | bytes 1540
  0.8 1.0 %copy-start.8 = (f32[256]{0:T(256)S(1)}, f32[256]{0:T(256)}, u32[]{:S(2)}) copy-start(f32[256]{0:T(256)} %param.19) | copy-start | bytes 3076
  0.8 1.0 %copy-start.9 = (f32[2,16]{1,0:T(2,128)S(1)}, f32[2,16]{1,0:T(2,128)}, u32[]{:S(2)}) copy-start(f32[2,16]{1,0:T(2,128)} %row_rate_ref.1) | copy-start | bytes 388
  0.8 1.0 %copy-start.10 = (f32[2,16]{1,0:T(2,128)S(1)}, f32[2,16]{1,0:T(2,128)}, u32[]{:S(2)}) copy-start(f32[2,16]{1,0:T(2,128)} %col_rate_ref.1) | copy-start | bytes 388
  0.8 1.0 %copy-start.11 = (f32[256]{0:T(256)S(1)}, f32[256]{0:T(256)}, u32[]{:S(2)}) copy-start(f32[256]{0:T(256)} %param.28) | copy-start | bytes 3076
  0.8 1.0 %copy-start.12 = (s32[8]{0:T(128)S(1)}, s32[8]{0:T(128)}, u32[]{:S(2)}) copy-start(s32[8]{0:T(128)} %trace_ref.1) | copy-start | bytes 100
  1.9 1.0 %copy-start = (bf16[256,1024]{1,0:T(8,128)(2,1)S(1)}, bf16[256,1024]{1,0:T(8,128)(2,1)}, u32[]{:S(2)}) copy-start(bf16[256,1024]{1,0:T(8,128)(2,1)} %bc_ref.1) | copy-start | bytes 1572868
  2.9 0.9 %copy-start.1 = (bf16[256,512]{1,0:T(8,128)(2,1)S(1)}, bf16[256,512]{1,0:T(8,128)(2,1)}, u32[]{:S(2)}) copy-start(bf16[256,512]{1,0:T(8,128)(2,1)} %in_ref.1) | copy-start | bytes 786436
  3.9 0.9 %copy-start.2 = (bf16[256,256]{1,0:T(8,128)(2,1)S(1)}, bf16[256,256]{1,0:T(8,128)(2,1)}, u32[]{:S(2)}) copy-start(bf16[256,256]{1,0:T(8,128)(2,1)} %cond_ref.1) | copy-start | bytes 393220
  4.8 0.9 %copy-start.3 = (bf16[256,256]{1,0:T(8,128)(2,1)S(1)}, bf16[256,256]{1,0:T(8,128)(2,1)}, u32[]{:S(2)}) copy-start(bf16[256,256]{1,0:T(8,128)(2,1)} %out_weight_ref.1) | copy-start | bytes 393220
